TPU v7x, 32 devices: a whole 2x2x4 slice. The times are simulated.
32 devices in a mesh: group: 4 (over x, core), head: 8 (over z, y).
Axes of the slice: x: 2, y: 2, z: 4, core: 2. Of those that a mesh axis runs over, the one named last changes fastest.
Arguments:
- queries: bfloat16 [4, 1024, 4096], P('group', 'head')
- keys: bfloat16 [4, 1024, 4096], P('group', 'head')
- values: bfloat16 [4, 1024, 4096], P('group', 'head'), may hold values from -6 to 6
- group_mask: int32 [4, 4, 32], replicated, may hold values from 0 to 1, as said below
- noise_level: int32 [4], replicated, may hold values from 0 to 7
- token_count: int32 [4], replicated, may hold values from 512 to 1024, as said below
- level_gate: float32 [8, 4096], replicated, may hold values from 0.5 to 2
Outputs:
- gated: bfloat16 [4, 1024, 4096], P('group', 'head')
Inputs may be any that keep to these rules, and one draw needn't show every extreme that they name: group_mask[c, c, h] = 1; group_mask[c, e, h] = 0 where e > c or c - e >= 3; the last group attends in every head to all 3 groups it may. `token_count`: some group has all 1024 tokens live.
All inputs are finite; a program needn't handle non-finite values.
Results may differ from a plain program's by a relative error of at most 0.0048.
Values may be sent and summed in bfloat16 or wider, within the bound.
A program may use at most 128 MiB of HBM per device.

v0:
```python
import functools
import math

import jax
import jax.numpy as jnp
from jax import lax
from jax.experimental import pallas as pl
from jax.experimental.pallas import tpu as pltpu
from jax.sharding import PartitionSpec as P

HD = 128
WIN = 3
AHEAD = 2
MESH = pl.DeviceIdType.MESH


def kernel(
    n, groups, tile,
    q_ref, k_ref, v_ref, mask_ref, level_ref, count_ref, gate_ref, out_ref,
    qbuf, kvbuf, slots, kall, vall, obuf,
    kv_send, kv_recv, q_send, q_recv, slot_send, slot_recv, out_send, out_recv,
):
    group = lax.axis_index("group")
    me = lax.axis_index("head")
    heads, seq, _ = qbuf.shape
    tokens = seq // n
    half = n // 2
    has_next = group < groups - 1
    per = tile // tokens
    n_tiles = seq // tile
    scale = HD ** -0.5 * math.log2(math.e)
    mine = pl.ds(pl.multiple_of(me * tokens, tokens), tokens)

    def columns(place, head):
        return pl.ds(pl.multiple_of((place * heads + head) * HD, HD), HD)

    barrier = pltpu.get_barrier_semaphore()

    def greet(step, carry):
        pl.semaphore_signal(
            barrier, inc=1, device_id={"head": lax.rem(me + step, n)}, device_id_type=MESH
        )
        return carry

    lax.fori_loop(1, n, greet, 0)

    @pl.when(has_next)
    def _():
        pl.semaphore_signal(barrier, inc=1, device_id={"group": group + 1}, device_id_type=MESH)

    @pl.when(group >= 1)
    def _():
        pl.semaphore_signal(barrier, inc=1, device_id={"group": group - 1}, device_id_type=MESH)

    beside = jnp.minimum(group, 1) + jnp.minimum(groups - 1 - group, 1)
    pl.semaphore_wait(barrier, n - 1 + beside)

    def scatter(head, pairs, send_sem, recv_sem):
        for source, target in pairs:
            pltpu.make_async_copy(
                source.at[0, :, columns(me, head)], target.at[mine, :], recv_sem
            ).start()

        def body(step, carry):
            odd = step % 2
            shift = odd * ((step + 1) // 2) + (1 - odd) * (half + step // 2)
            place = lax.rem(me + shift, n)
            for source, target in pairs:
                pltpu.make_async_remote_copy(
                    src_ref=source.at[0, :, columns(place, head)],
                    dst_ref=target.at[mine, :],
                    send_sem=send_sem,
                    recv_sem=recv_sem,
                    device_id={"head": place},
                    device_id_type=MESH,
                ).start()
            return carry

        lax.fori_loop(0, n - 1, body, 0)

    def send_head(head):
        scatter(
            head,
            ((k_ref, kvbuf.at[head, 0]), (v_ref, kvbuf.at[head, 1])),
            kv_send.at[head],
            kv_recv.at[head],
        )
        scatter(head, ((q_ref, qbuf.at[head]),), q_send.at[head], q_recv.at[head])

    def wait_sent(head):
        sent = pl.ds(0, (n - 1) * tokens)
        kv = kvbuf.at[head, :, sent, :]
        pltpu.make_async_copy(kv, kv, kv_send.at[head]).wait()
        q = qbuf.at[head, sent, :]
        pltpu.make_async_copy(q, q, q_send.at[head]).wait()

    def hand_on(head, slot):
        return pltpu.make_async_remote_copy(
            src_ref=kvbuf.at[head] if slot == 0 else slots.at[slot - 1, head],
            dst_ref=slots.at[slot, head],
            send_sem=slot_send.at[slot, head],
            recv_sem=slot_recv.at[slot, head],
            device_id={"group": group + 1},
            device_id_type=MESH,
        )

    def compute(head):
        head_number = me * heads + head
        first_key = kvbuf[head, 0, 0:16, :].astype(jnp.float32)[0:1, :]
        positions = lax.broadcasted_iota(jnp.int32, (seq, HD), 0)
        for offset in range(WIN):
            source = jnp.maximum(group - offset, 0)
            live = jnp.where(
                group >= offset, count_ref[source] * mask_ref[group, source, head_number], 0
            )
            valid = positions < live
            block = kvbuf.at[head] if offset == 0 else slots.at[offset - 1, head]
            rows = pl.ds(offset * seq, seq)
            kall[rows, :] = jnp.where(
                valid, block[0].astype(jnp.float32), first_key
            ).astype(jnp.bfloat16)
            vall[rows, 0:HD] = jnp.where(valid, block[1].astype(jnp.float32), 0.0).astype(
                jnp.bfloat16
            )
            vall[rows, HD : 2 * HD] = jnp.where(valid, 1.0, 0.0).astype(jnp.bfloat16)
        gates = gate_ref[:, columns(me, head)]
        levels = lax.broadcasted_iota(jnp.int32, gates.shape, 0)
        gate = jnp.sum(
            jnp.where(levels == level_ref[group], gates, 0.0), axis=0, keepdims=True
        )

        def body(step, carry):
            index = lax.rem(step + me // per + n_tiles // 2, n_tiles)
            start = pl.multiple_of(index * tile, tile)
            scores = lax.dot_general(
                qbuf[head, pl.ds(start, tile), :],
                kall[...],
                (((1,), (1,)), ((), ())),
                preferred_element_type=jnp.float32,
            )
            top = jnp.max(scores, axis=1, keepdims=True)
            weights = jnp.exp2((scores - top) * scale).astype(jnp.bfloat16)
            summed = jnp.dot(weights, vall[...], preferred_element_type=jnp.float32)
            gated = summed[:, 0:HD] / summed[:, HD : 2 * HD] * gate
            obuf[head, pl.ds(start, tile), :] = gated.astype(jnp.bfloat16)
            for piece in range(per):
                place = index * per + piece
                piece_rows = pl.ds(pl.multiple_of(place * tokens, tokens), tokens)
                finished = obuf.at[head, piece_rows, :]
                landing = out_ref.at[0, :, columns(me, head)]

                @pl.when(place == me)
                def _():
                    pltpu.make_async_copy(finished, landing, out_recv).start()

                @pl.when(place != me)
                def _():
                    pltpu.make_async_remote_copy(
                        src_ref=finished,
                        dst_ref=landing,
                        send_sem=out_send,
                        recv_sem=out_recv,
                        device_id={"head": place},
                        device_id_type=MESH,
                    ).start()

            return carry

        lax.fori_loop(0, n_tiles, body, 0)

    for head in range(min(AHEAD, heads)):
        send_head(head)
    for stage in range(heads + 1):
        if stage < heads:
            pltpu.make_async_copy(kvbuf.at[stage], kvbuf.at[stage], kv_recv.at[stage]).wait()

            @pl.when(has_next)
            def _():
                hand_on(stage, 0).start()

            if stage + AHEAD < heads:
                wait_sent(stage)
                send_head(stage + AHEAD)

            @pl.when(group >= 1)
            def _():
                hand_on(stage, 0).wait_recv()

                @pl.when(has_next)
                def _():
                    hand_on(stage, 1).start()

        if stage >= 1:
            head = stage - 1
            pltpu.make_async_copy(qbuf.at[head], qbuf.at[head], q_recv.at[head]).wait()

            @pl.when(group >= 2)
            def _():
                hand_on(head, 1).wait_recv()

            compute(head)

    for head in range(heads):
        if head + AHEAD >= heads:
            wait_sent(head)

        @pl.when(has_next)
        def _():
            hand_on(head, 0).wait_send()

            @pl.when(group >= 1)
            def _():
                hand_on(head, 1).wait_send()

    sent = obuf.at[:, pl.ds(0, (n - 1) * tokens), :]
    pltpu.make_async_copy(sent, sent, out_send).wait()
    pltpu.make_async_copy(out_ref, out_ref, out_recv).wait()


def solution(mesh):
    n = mesh.shape["head"]
    groups = mesh.shape["group"]

    def shards(queries, keys, values, group_mask, noise_level, token_count, level_gate):
        _, tokens, features = queries.shape
        heads = features // HD // n
        seq = tokens * n
        tile = max(tokens, 256 if seq <= 1024 else 128)
        any_space = pl.BlockSpec(memory_space=pl.ANY)
        smem = pl.BlockSpec(memory_space=pltpu.SMEM)
        dma = pltpu.SemaphoreType.DMA
        scores = heads * seq * seq * WIN
        return pl.pallas_call(
            functools.partial(kernel, n, groups, tile),
            out_shape=jax.ShapeDtypeStruct(queries.shape, jnp.bfloat16),
            in_specs=[any_space] * 3 + [smem] * 3 + [pl.BlockSpec(memory_space=pltpu.VMEM)],
            out_specs=any_space,
            scratch_shapes=[
                pltpu.VMEM((heads, seq, HD), jnp.bfloat16),
                pltpu.VMEM((heads, 2, seq, HD), jnp.bfloat16),
                pltpu.VMEM((WIN - 1, heads, 2, seq, HD), jnp.bfloat16),
                pltpu.VMEM((WIN * seq, HD), jnp.bfloat16),
                pltpu.VMEM((WIN * seq, 2 * HD), jnp.bfloat16),
                pltpu.VMEM((heads, seq, HD), jnp.bfloat16),
                dma((heads,)),
                dma((heads,)),
                dma((heads,)),
                dma((heads,)),
                dma((WIN - 1, heads)),
                dma((WIN - 1, heads)),
                dma,
                dma,
            ],
            compiler_params=pltpu.CompilerParams(
                collective_id=0, has_side_effects=True, vmem_limit_bytes=56 * 1024 * 1024
            ),
            cost_estimate=pl.CostEstimate(
                flops=scores * HD * 4, bytes_accessed=queries.size * 8, transcendentals=scores
            ),
        )(queries, keys, values, group_mask, noise_level, token_count, level_gate)

    return jax.shard_map(
        shards,
        mesh=mesh,
        in_specs=(P("group", "head", None),) * 3 + (P(),) * 4,
        out_specs=P("group", "head", None),
        check_vma=False,
    )
```

profile of v0, /device:TPU:6, one launch (start us, length us, event | category | flops | bytes accessed | tf_op | source)
XLA Modules:
  0.0 108.4 jit_solution(13275966104285310208)
XLA Ops:
  0.0 106.1 %shard_map.73 = bf16[1,128,4096]{2,1,0:T(8,128)(2,1)} custom-call(bf16[1,128,4096]{2,1,0:T(8,128)(2,1)} %q_ref.1, bf16[1,128,4096]{2,1,0:T(8,128)(2,1)} %k_ref.1, bf16[1,128,4096]{2,1,0:T(8,128)(2,1)} %v_ref.1, s32[4,4,32]{2,1,0:T(4,128)} %mask_ref.1, s32[4]{0:T(128)} %level_ref.1, s32[4]{0:T(128)} %count_ref.1, f32[8,4096]{1,0:T(8,128)} %gate_ref.1), custom_call_target="tpu_custom_call" | custom-call | flops 6442450944 | bytes 4194304 | tf_op jit(solution)/shard_map/pallas_call | solution.py:233
  106.1 2.3 %copy.9 = bf16[1,128,4096]{2,1,0:T(8,128)(2,1)} copy(bf16[1,128,4096]{2,1,0:T(8,128)(2,1)} %shard_map.73) | data formatting | bytes 2097152
where the time goes:
time: 109 us; the launch traced here: 108 us
  Pallas kernels  106 us (97%)
  local copies, waits for them, and re-layouts  2.29 us (2%)
    pallas_call x1, Pallas kernels, shards(): pl.pallas_call(functools.partial(kernel, n, groups, tile), out_shape=jax....  106 us
    unnamed x1, local copies, waits for them, and re-layouts  2.29 us

commit v1 on v0

--- a/solution.py
+++ b/solution.py
@@ -10,7 +10,7 @@
 
 HD = 128
 WIN = 3
-AHEAD = 2
+AHEAD = 4
 MESH = pl.DeviceIdType.MESH
 
 

time: 109 us -> 109 us (level)
  no operation moved by 1% of the time
where the time goes in v1:
time: 109 us; the launch traced here: 108 us
  Pallas kernels  106 us (97%)
  local copies, waits for them, and re-layouts  2.29 us (2%)
    pallas_call x1, Pallas kernels, shards(): pl.pallas_call(functools.partial(kernel, n, groups, tile), out_shape=jax....  106 us
    unnamed x1, local copies, waits for them, and re-layouts  2.29 us

profile of v1, /device:TPU:6, one launch (start us, length us, event | category | flops | bytes accessed | tf_op | source)
XLA Modules:
  0.0 108.4 jit_solution(15815245592564383101)
XLA Ops:
  0.0 106.1 %shard_map.73 = bf16[1,128,4096]{2,1,0:T(8,128)(2,1)} custom-call(bf16[1,128,4096]{2,1,0:T(8,128)(2,1)} %q_ref.1, bf16[1,128,4096]{2,1,0:T(8,128)(2,1)} %k_ref.1, bf16[1,128,4096]{2,1,0:T(8,128)(2,1)} %v_ref.1, s32[4,4,32]{2,1,0:T(4,128)} %mask_ref.1, s32[4]{0:T(128)} %level_ref.1, s32[4]{0:T(128)} %count_ref.1, f32[8,4096]{1,0:T(8,128)} %gate_ref.1), custom_call_target="tpu_custom_call" | custom-call | flops 6442450944 | bytes 4194304 | tf_op jit(solution)/shard_map/pallas_call | solution.py:233
  106.1 2.3 %copy.9 = bf16[1,128,4096]{2,1,0:T(8,128)(2,1)} copy(bf16[1,128,4096]{2,1,0:T(8,128)(2,1)} %shard_map.73) | data formatting | bytes 2097152

commit v2 on v1

--- a/solution.py
+++ b/solution.py
@@ -104,7 +104,7 @@
             device_id_type=MESH,
         )
 
-    def compute(head):
+    def prepare(head):
         head_number = me * heads + head
         first_key = kvbuf[head, 0, 0:16, :].astype(jnp.float32)[0:1, :]
         positions = lax.broadcasted_iota(jnp.int32, (seq, HD), 0)
@@ -123,6 +123,8 @@
                 jnp.bfloat16
             )
             vall[rows, HD : 2 * HD] = jnp.where(valid, 1.0, 0.0).astype(jnp.bfloat16)
+
+    def attend(head, first, last):
         gates = gate_ref[:, columns(me, head)]
         levels = lax.broadcasted_iota(jnp.int32, gates.shape, 0)
         gate = jnp.sum(
@@ -132,15 +134,22 @@
         def body(step, carry):
             index = lax.rem(step + me // per + n_tiles // 2, n_tiles)
             start = pl.multiple_of(index * tile, tile)
-            scores = lax.dot_general(
-                qbuf[head, pl.ds(start, tile), :],
-                kall[...],
-                (((1,), (1,)), ((), ())),
-                preferred_element_type=jnp.float32,
+            rows = qbuf[head, pl.ds(start, tile), :]
+            tops, sums = [], []
+            for offset in range(WIN):
+                keys = pl.ds(offset * seq, seq)
+                scores = lax.dot_general(
+                    rows, kall[keys, :], (((1,), (1,)), ((), ())),
+                    preferred_element_type=jnp.float32,
+                )
+                top = jnp.max(scores, axis=1, keepdims=True)
+                weights = jnp.exp2((scores - top) * scale).astype(jnp.bfloat16)
+                tops.append(top)
+                sums.append(jnp.dot(weights, vall[keys, :], preferred_element_type=jnp.float32))
+            joint = functools.reduce(jnp.maximum, tops)
+            summed = sum(
+                jnp.exp2((top - joint) * scale) * part for top, part in zip(tops, sums)
             )
-            top = jnp.max(scores, axis=1, keepdims=True)
-            weights = jnp.exp2((scores - top) * scale).astype(jnp.bfloat16)
-            summed = jnp.dot(weights, vall[...], preferred_element_type=jnp.float32)
             gated = summed[:, 0:HD] / summed[:, HD : 2 * HD] * gate
             obuf[head, pl.ds(start, tile), :] = gated.astype(jnp.bfloat16)
             for piece in range(per):
@@ -166,11 +175,12 @@
 
             return carry
 
-        lax.fori_loop(0, n_tiles, body, 0)
+        lax.fori_loop(first, last, body, 0)
 
     for head in range(min(AHEAD, heads)):
         send_head(head)
     for stage in range(heads + 1):
+        head = stage - 1
         if stage < heads:
             pltpu.make_async_copy(kvbuf.at[stage], kvbuf.at[stage], kv_recv.at[stage]).wait()
 
@@ -182,6 +192,18 @@
                 wait_sent(stage)
                 send_head(stage + AHEAD)
 
+        if stage >= 1:
+            pltpu.make_async_copy(qbuf.at[head], qbuf.at[head], q_recv.at[head]).wait()
+
+            @pl.when(group >= 2)
+            def _():
+                hand_on(head, 1).wait_recv()
+
+            prepare(head)
+            attend(head, 0, n_tiles // 2)
+
+        if stage < heads:
+
             @pl.when(group >= 1)
             def _():
                 hand_on(stage, 0).wait_recv()
@@ -191,14 +213,7 @@
                     hand_on(stage, 1).start()
 
         if stage >= 1:
-            head = stage - 1
-            pltpu.make_async_copy(qbuf.at[head], qbuf.at[head], q_recv.at[head]).wait()
-
-            @pl.when(group >= 2)
-            def _():
-                hand_on(head, 1).wait_recv()
-
-            compute(head)
+            attend(head, n_tiles // 2, n_tiles)
 
     for head in range(heads):
         if head + AHEAD >= heads:

time: 109 us -> 103 us (0.945)
  Pallas kernels: 106 us -> 100 us
    pallas_call x1, Pallas kernels: 106 us -> 100 us  [shards(): pl.pallas_call(functools.partial(kernel, n, groups, tile), out_shape=jax....]
where the time goes in v2:
time: 103 us
  Pallas kernels  100 us (97%)
  local copies, waits for them, and re-layouts  2.29 us (2%)
    pallas_call x1, Pallas kernels, shards(): pl.pallas_call(functools.partial(kernel, n, groups, tile), out_shape=jax....  100 us
    unnamed x1, local copies, waits for them, and re-layouts  2.29 us

profile of v2, /device:TPU:6, one launch (start us, length us, event | category | flops | bytes accessed | tf_op | source)
XLA Modules:
  0.0 102.8 jit_solution(16524328447492991397)
XLA Ops:
  0.0 100.5 %shard_map.73 = bf16[1,128,4096]{2,1,0:T(8,128)(2,1)} custom-call(bf16[1,128,4096]{2,1,0:T(8,128)(2,1)} %q_ref.1, bf16[1,128,4096]{2,1,0:T(8,128)(2,1)} %k_ref.1, bf16[1,128,4096]{2,1,0:T(8,128)(2,1)} %v_ref.1, s32[4,4,32]{2,1,0:T(4,128)} %mask_ref.1, s32[4]{0:T(128)} %level_ref.1, s32[4]{0:T(128)} %count_ref.1, f32[8,4096]{1,0:T(8,128)} %gate_ref.1), custom_call_target="tpu_custom_call" | custom-call | flops 6442450944 | bytes 4194304 | tf_op jit(solution)/shard_map/pallas_call | solution.py:248
  100.5 2.3 %copy.9 = bf16[1,128,4096]{2,1,0:T(8,128)(2,1)} copy(bf16[1,128,4096]{2,1,0:T(8,128)(2,1)} %shard_map.73) | data formatting | bytes 2097152

commit v3 on v2

--- a/solution.py
+++ b/solution.py
@@ -10,7 +10,6 @@
 
 HD = 128
 WIN = 3
-AHEAD = 4
 MESH = pl.DeviceIdType.MESH
 
 
@@ -78,13 +77,15 @@
 
         lax.fori_loop(0, n - 1, body, 0)
 
-    def send_head(head):
+    def send_keys(head):
         scatter(
             head,
             ((k_ref, kvbuf.at[head, 0]), (v_ref, kvbuf.at[head, 1])),
             kv_send.at[head],
             kv_recv.at[head],
         )
+
+    def send_queries(head):
         scatter(head, ((q_ref, qbuf.at[head]),), q_send.at[head], q_recv.at[head])
 
     def wait_sent(head):
@@ -177,8 +178,11 @@
 
         lax.fori_loop(first, last, body, 0)
 
-    for head in range(min(AHEAD, heads)):
-        send_head(head)
+    send_keys(0)
+    for head in range(heads):
+        if head + 1 < heads:
+            send_keys(head + 1)
+        send_queries(head)
     for stage in range(heads + 1):
         head = stage - 1
         if stage < heads:
@@ -188,10 +192,6 @@
             def _():
                 hand_on(stage, 0).start()
 
-            if stage + AHEAD < heads:
-                wait_sent(stage)
-                send_head(stage + AHEAD)
-
         if stage >= 1:
             pltpu.make_async_copy(qbuf.at[head], qbuf.at[head], q_recv.at[head]).wait()
 
@@ -216,8 +216,7 @@
             attend(head, n_tiles // 2, n_tiles)
 
     for head in range(heads):
-        if head + AHEAD >= heads:
-            wait_sent(head)
+        wait_sent(head)
 
         @pl.when(has_next)
         def _():

time: 103 us -> 100 us (0.971)
  Pallas kernels: 100 us -> 97.9 us
    pallas_call x1, Pallas kernels: 100 us -> 97.9 us  [shards(): pl.pallas_call(functools.partial(kernel, n, groups, tile), out_shape=jax....]
where the time goes in v3:
time: 100 us
  Pallas kernels  97.9 us (98%)
  local copies, waits for them, and re-layouts  2.29 us (2%)
    pallas_call x1, Pallas kernels, shards(): pl.pallas_call(functools.partial(kernel, n, groups, tile), out_shape=jax....  97.9 us
    unnamed x1, local copies, waits for them, and re-layouts  2.29 us

profile of v3, /device:TPU:6, one launch (start us, length us, event | category | flops | bytes accessed | tf_op | source)
XLA Modules:
  0.0 100.2 jit_solution(4835494100498119698)
XLA Ops:
  0.0 97.9 %shard_map.73 = bf16[1,128,4096]{2,1,0:T(8,128)(2,1)} custom-call(bf16[1,128,4096]{2,1,0:T(8,128)(2,1)} %q_ref.1, bf16[1,128,4096]{2,1,0:T(8,128)(2,1)} %k_ref.1, bf16[1,128,4096]{2,1,0:T(8,128)(2,1)} %v_ref.1, s32[4,4,32]{2,1,0:T(4,128)} %mask_ref.1, s32[4]{0:T(128)} %level_ref.1, s32[4]{0:T(128)} %count_ref.1, f32[8,4096]{1,0:T(8,128)} %gate_ref.1), custom_call_target="tpu_custom_call" | custom-call | flops 6442450944 | bytes 4194304 | tf_op jit(solution)/shard_map/pallas_call | solution.py:247
  97.9 2.3 %copy.9 = bf16[1,128,4096]{2,1,0:T(8,128)(2,1)} copy(bf16[1,128,4096]{2,1,0:T(8,128)(2,1)} %shard_map.73) | data formatting | bytes 2097152

commit v4 on v3

--- a/solution.py
+++ b/solution.py
@@ -124,6 +124,29 @@
                 jnp.bfloat16
             )
             vall[rows, HD : 2 * HD] = jnp.where(valid, 1.0, 0.0).astype(jnp.bfloat16)
+
+    def held_back(head):
+        return head + 2 < heads
+
+    def send_result(head, place):
+        rows = pl.ds(pl.multiple_of(place * tokens, tokens), tokens)
+        finished = obuf.at[head, rows, :]
+        landing = out_ref.at[0, :, columns(me, head)]
+
+        @pl.when(place == me)
+        def _():
+            pltpu.make_async_copy(finished, landing, out_recv).start()
+
+        @pl.when(place != me)
+        def _():
+            pltpu.make_async_remote_copy(
+                src_ref=finished,
+                dst_ref=landing,
+                send_sem=out_send,
+                recv_sem=out_recv,
+                device_id={"head": place},
+                device_id_type=MESH,
+            ).start()
 
     def attend(head, first, last):
         gates = gate_ref[:, columns(me, head)]
@@ -153,27 +176,9 @@
             )
             gated = summed[:, 0:HD] / summed[:, HD : 2 * HD] * gate
             obuf[head, pl.ds(start, tile), :] = gated.astype(jnp.bfloat16)
-            for piece in range(per):
-                place = index * per + piece
-                piece_rows = pl.ds(pl.multiple_of(place * tokens, tokens), tokens)
-                finished = obuf.at[head, piece_rows, :]
-                landing = out_ref.at[0, :, columns(me, head)]
-
-                @pl.when(place == me)
-                def _():
-                    pltpu.make_async_copy(finished, landing, out_recv).start()
-
-                @pl.when(place != me)
-                def _():
-                    pltpu.make_async_remote_copy(
-                        src_ref=finished,
-                        dst_ref=landing,
-                        send_sem=out_send,
-                        recv_sem=out_recv,
-                        device_id={"head": place},
-                        device_id_type=MESH,
-                    ).start()
-
+            if not held_back(head):
+                for piece in range(per):
+                    send_result(head, index * per + piece)
             return carry
 
         lax.fori_loop(first, last, body, 0)
@@ -214,6 +219,16 @@
 
         if stage >= 1:
             attend(head, n_tiles // 2, n_tiles)
+
+        if stage == heads - 1:
+            for early in range(heads):
+                if held_back(early):
+
+                    def body(step, carry):
+                        send_result(early, lax.rem(me + half + step, n))
+                        return carry
+
+                    lax.fori_loop(0, n, body, 0)
 
     for head in range(heads):
         wait_sent(head)

time: 100 us -> 101 us (1.010); the launches traced: 100 us -> 99.8 us
  no operation moved by 1% of the time
where the time goes in v4:
time: 101 us; the launch traced here: 99.8 us
  Pallas kernels  97.5 us (97%)
  local copies, waits for them, and re-layouts  2.29 us (2%)
    pallas_call x1, Pallas kernels, shards(): pl.pallas_call(functools.partial(kernel, n, groups, tile), out_shape=jax....  97.5 us
    unnamed x1, local copies, waits for them, and re-layouts  2.29 us

profile of v4, /device:TPU:6, one launch (start us, length us, event | category | flops | bytes accessed | tf_op | source)
XLA Modules:
  0.0 99.8 jit_solution(1309307308488223559)
XLA Ops:
  0.0 97.5 %shard_map.73 = bf16[1,128,4096]{2,1,0:T(8,128)(2,1)} custom-call(bf16[1,128,4096]{2,1,0:T(8,128)(2,1)} %q_ref.1, bf16[1,128,4096]{2,1,0:T(8,128)(2,1)} %k_ref.1, bf16[1,128,4096]{2,1,0:T(8,128)(2,1)} %v_ref.1, s32[4,4,32]{2,1,0:T(4,128)} %mask_ref.1, s32[4]{0:T(128)} %level_ref.1, s32[4]{0:T(128)} %count_ref.1, f32[8,4096]{1,0:T(8,128)} %gate_ref.1), custom_call_target="tpu_custom_call" | custom-call | flops 6442450944 | bytes 4194304 | tf_op jit(solution)/shard_map/pallas_call | solution.py:262
  97.5 2.3 %copy.9 = bf16[1,128,4096]{2,1,0:T(8,128)(2,1)} copy(bf16[1,128,4096]{2,1,0:T(8,128)(2,1)} %shard_map.73) | data formatting | bytes 2097152

commit v5 on v3

--- a/solution.py
+++ b/solution.py
@@ -54,6 +54,12 @@
     beside = jnp.minimum(group, 1) + jnp.minimum(groups - 1 - group, 1)
     pl.semaphore_wait(barrier, n - 1 + beside)
 
+    def partner(shift):
+        if n & (n - 1):
+            return lax.rem(me + shift, n)
+        bits = [1 << power for power in range(n.bit_length() - 1)]
+        return sum((me // bit + shift // bit) % 2 * bit for bit in bits)
+
     def scatter(head, pairs, send_sem, recv_sem):
         for source, target in pairs:
             pltpu.make_async_copy(
@@ -63,7 +69,7 @@
         def body(step, carry):
             odd = step % 2
             shift = odd * ((step + 1) // 2) + (1 - odd) * (half + step // 2)
-            place = lax.rem(me + shift, n)
+            place = partner(shift)
             for source, target in pairs:
                 pltpu.make_async_remote_copy(
                     src_ref=source.at[0, :, columns(place, head)],

time: 100 us -> 100 us (level); the launches traced: 100 us -> 98.9 us
  Pallas kernels: 97.9 us -> 96.6 us
    pallas_call x1, Pallas kernels: 97.9 us -> 96.6 us  [shards(): pl.pallas_call(functools.partial(kernel, n, groups, tile), out_shape=jax....]
where the time goes in v5:
time: 100 us; the launch traced here: 98.9 us
  Pallas kernels  96.6 us (97%)
  local copies, waits for them, and re-layouts  2.29 us (2%)
    pallas_call x1, Pallas kernels, shards(): pl.pallas_call(functools.partial(kernel, n, groups, tile), out_shape=jax....  96.6 us
    unnamed x1, local copies, waits for them, and re-layouts  2.29 us

profile of v5, /device:TPU:6, one launch (start us, length us, event | category | flops | bytes accessed | tf_op | source)
XLA Modules:
  0.0 98.9 jit_solution(12495611294952363555)
XLA Ops:
  0.0 96.6 %shard_map.73 = bf16[1,128,4096]{2,1,0:T(8,128)(2,1)} custom-call(bf16[1,128,4096]{2,1,0:T(8,128)(2,1)} %q_ref.1, bf16[1,128,4096]{2,1,0:T(8,128)(2,1)} %k_ref.1, bf16[1,128,4096]{2,1,0:T(8,128)(2,1)} %v_ref.1, s32[4,4,32]{2,1,0:T(4,128)} %mask_ref.1, s32[4]{0:T(128)} %level_ref.1, s32[4]{0:T(128)} %count_ref.1, f32[8,4096]{1,0:T(8,128)} %gate_ref.1), custom_call_target="tpu_custom_call" | custom-call | flops 6442450944 | bytes 4194304 | tf_op jit(solution)/shard_map/pallas_call | solution.py:253
  96.6 2.3 %copy.9 = bf16[1,128,4096]{2,1,0:T(8,128)(2,1)} copy(bf16[1,128,4096]{2,1,0:T(8,128)(2,1)} %shard_map.73) | data formatting | bytes 2097152

commit v6 on v5

--- a/solution.py
+++ b/solution.py
@@ -132,6 +132,17 @@
             vall[rows, HD : 2 * HD] = jnp.where(valid, 1.0, 0.0).astype(jnp.bfloat16)
 
     def attend(head, first, last):
+        if head + 2 < heads:
+            attend_blocks(head, first, last, WIN)
+            return
+        reach = jnp.minimum(group, WIN - 1)
+        for blocks in range(1, WIN + 1):
+
+            @pl.when(reach == blocks - 1)
+            def _():
+                attend_blocks(head, first, last, blocks)
+
+    def attend_blocks(head, first, last, blocks):
         gates = gate_ref[:, columns(me, head)]
         levels = lax.broadcasted_iota(jnp.int32, gates.shape, 0)
         gate = jnp.sum(
@@ -143,7 +154,7 @@
             start = pl.multiple_of(index * tile, tile)
             rows = qbuf[head, pl.ds(start, tile), :]
             tops, sums = [], []
-            for offset in range(WIN):
+            for offset in range(blocks):
                 keys = pl.ds(offset * seq, seq)
                 scores = lax.dot_general(
                     rows, kall[keys, :], (((1,), (1,)), ((), ())),
@@ -206,7 +217,7 @@
                 hand_on(head, 1).wait_recv()
 
             prepare(head)
-            attend(head, 0, n_tiles // 2)
+            attend(head, 0, n_tiles // 2 if stage < heads else n_tiles)
 
         if stage < heads:
 
@@ -218,8 +229,8 @@
                 def _():
                     hand_on(stage, 1).start()
 
-        if stage >= 1:
-            attend(head, n_tiles // 2, n_tiles)
+            if stage >= 1:
+                attend(head, n_tiles // 2, n_tiles)
 
     for head in range(heads):
         wait_sent(head)

time: 100 us -> 100 us (level)
  no operation moved by 1% of the time
where the time goes in v6:
time: 100 us; the launch traced here: 98.7 us
  Pallas kernels  96.4 us (96%)
  local copies, waits for them, and re-layouts  2.29 us (2%)
    pallas_call x1, Pallas kernels, shards(): pl.pallas_call(functools.partial(kernel, n, groups, tile), out_shape=jax....  96.4 us
    unnamed x1, local copies, waits for them, and re-layouts  2.29 us

profile of v6, /device:TPU:6, one launch (start us, length us, event | category | flops | bytes accessed | tf_op | source)
XLA Modules:
  0.0 98.7 jit_solution(13736271209003602704)
XLA Ops:
  0.0 96.4 %shard_map.73 = bf16[1,128,4096]{2,1,0:T(8,128)(2,1)} custom-call(bf16[1,128,4096]{2,1,0:T(8,128)(2,1)} %q_ref.1, bf16[1,128,4096]{2,1,0:T(8,128)(2,1)} %k_ref.1, bf16[1,128,4096]{2,1,0:T(8,128)(2,1)} %v_ref.1, s32[4,4,32]{2,1,0:T(4,128)} %mask_ref.1, s32[4]{0:T(128)} %level_ref.1, s32[4]{0:T(128)} %count_ref.1, f32[8,4096]{1,0:T(8,128)} %gate_ref.1), custom_call_target="tpu_custom_call" | custom-call | flops 6442450944 | bytes 4194304 | tf_op jit(solution)/shard_map/pallas_call | solution.py:264
  96.4 2.3 %copy.9 = bf16[1,128,4096]{2,1,0:T(8,128)(2,1)} copy(bf16[1,128,4096]{2,1,0:T(8,128)(2,1)} %shard_map.73) | data formatting | bytes 2097152
